TPU v7x, 32 devices: a whole 2x2x4 slice. The times are simulated.
32 devices in a mesh: row: 4 (over x, core), col: 8 (over z, y).
Axes of the slice: x: 2, y: 2, z: 4, core: 2. Of those that a mesh axis runs over, the one named last changes fastest.
Arguments:
- blocks: bfloat16 [96, 16, 1024], P(('row', 'col')), may hold values from -1.5 to 1.5
- tile_ids: int32 [96, 8], P(('row', 'col')), may hold values from 0 to 127, all different within a row
- barrier: float32 [16384], P('row'), may hold values from 0.5 to 4
Outputs:
- panels: float32 [16384, 256], P('row')
- schur_rest: float32 [16384, 16384], P('row', 'col')
Inputs may be any that keep to these rules, and one draw needn't show every extreme that they name: `tile_ids`: each commodity lists 8 different arc tiles, and every tile is listed by some commodity.
All inputs are finite; a program needn't handle non-finite values.
Results may differ from a plain program's by a relative error of at most 0.0015.
Values may be sent and summed in bfloat16 or wider, within the bound.
A program may use at most 128 MiB of HBM per device.

v0:
```python
import jax
import jax.numpy as jnp
from jax import lax
from jax.sharding import PartitionSpec as P

TILE = 128
BT = 8
PANEL = 128
PANELS = 2


def spread_2(x, axis, root):
    mine = lax.axis_index(axis) == root
    return lax.psum(jnp.where(mine, x, jnp.zeros_like(x)), axis)


def expand(tiled, tile_list, first_tile, tile_count):
    wanted = first_tile + jnp.arange(tile_count, dtype=jnp.int32)
    onehot = (tile_list[:, :, None] == wanted[None, None, :]).astype(jnp.bfloat16)
    spread = jnp.einsum("kas,kjai->kjsi", onehot, tiled, preferred_element_type=jnp.float32)
    return spread.astype(jnp.bfloat16).reshape(
        tiled.shape[0] * tiled.shape[1], tile_count * tiled.shape[3]
    )


def shards(blocks, tile_ids, barrier):
    band_rows = barrier.shape[0]
    band_cols = band_rows * lax.axis_size("row") // lax.axis_size("col")
    row_at = lax.axis_index("row")
    col_at = lax.axis_index("col")
    row_tiles = band_rows // TILE
    col_tiles = band_cols // TILE
    row_glob = row_at * band_rows + jnp.arange(band_rows, dtype=jnp.int32)
    col_glob = col_at * band_cols + jnp.arange(band_cols, dtype=jnp.int32)
    initial = jnp.where(row_glob[:, None] == col_glob[None, :], barrier[:, None], 0.0)
    block_part = lax.all_gather(blocks, ("row", "col"), axis=0, tiled=True)
    tile_part = lax.all_gather(tile_ids, ("row", "col"), axis=0, tiled=True)
    tiled = block_part.reshape(block_part.shape[0], block_part.shape[1], BT, TILE)
    row_side = expand(tiled, tile_part, row_at * row_tiles, row_tiles)
    col_side = expand(tiled, tile_part, col_at * col_tiles, col_tiles)
    schur_tile = initial + lax.dot_general(
        row_side, col_side, (((0,), (0,)), ((), ())), preferred_element_type=jnp.float32
    )
    panel_list = []
    for panel_index in range(PANELS):
        low_edge = panel_index * PANEL
        high_edge = low_edge + PANEL
        own_cols = schur_tile[:, low_edge:high_edge]
        column = spread_2(own_cols, "col", 0)
        corner = spread_2(column[low_edge:high_edge], "row", 0)
        factor = jnp.linalg.cholesky(corner)
        solved = jax.scipy.linalg.solve_triangular(factor, column.T, lower=True).T
        placed = lax.dynamic_update_slice(
            jnp.zeros((band_rows, PANEL), jnp.float32), factor, (low_edge, 0)
        )
        panel_now = jnp.where(
            (row_glob < low_edge)[:, None],
            0.0,
            jnp.where((row_glob < high_edge)[:, None], placed, solved),
        )
        gathered = lax.all_gather(panel_now.astype(jnp.bfloat16), "row", axis=0, tiled=True).astype(
            panel_now.dtype
        )
        across = lax.dynamic_slice_in_dim(gathered, col_at * band_cols, band_cols, 0)
        update = lax.dot_general(
            panel_now, across, (((1,), (1,)), ((), ())), precision=lax.Precision.HIGHEST
        )
        inside = (row_glob >= high_edge)[:, None] & (col_glob >= high_edge)[None, :]
        schur_tile = schur_tile - jnp.where(inside, update, 0.0)
        panel_list.append(panel_now)
    return (jnp.concatenate(panel_list, axis=1), schur_tile)


def solution(mesh):
    placed = (P(("row", "col"), None, None), P(("row", "col"), None), P("row"))
    return jax.shard_map(
        shards,
        mesh=mesh,
        in_specs=placed,
        out_specs=(P("row", None), P("row", "col")),
        check_vma=False,
    )
```

profile of v0, /device:TPU:9, one launch (start us, length us, event | category | flops | bytes accessed | tf_op | source)
XLA Modules:
  0.0 623.4 jit_solution(2057977783166699046)
XLA Ops:
  7.2 0.7 all-gather.5.cloned.1.call-update
  8.0 58.6 %all-gather = s32[32,3,8]{2,1,0:T(4,128)S(1)} all-gather(s32[1,3,8]{2,1,0:T(4,128)} %bitcast.86), channel_id=1, replica_groups=mesh['row'=4,'col'=8] {'row','col'}, dimensions={0}, use_global_device_ids=true | all-gather | bytes 3168 | tf_op jit(solution)/shard_map/all_gather | solution.py:37
  66.7 4.1 all-gather.5.cloned.1.call-done
  70.7 2.7 copy.27
  73.5 6.1 convolution_convert_fusion
  79.6 4.8 convolution_convert_fusion.1
  84.4 54.4 %select_add_fusion = f32[4096,2048]{1,0:T(8,128)} fusion(f32[4096]{0:T(1024)S(1)} %copy-done, s32[2048]{0:T(1024)S(1)} %iota_add_fusion.1, s32[4096]{0:T(1024)S(1)} %iota_add_fusion, bf16[192,8,32,128]{3,2,1,0:T(8,128)(2,1)S(1)} %bitcast.83, bf16[192,8,16,128]{3,2,1,0:T(8,128)(2,1)} %bitcast.84), kind=kOutput, calls=%fused_computation.2 | convolution fusion | flops 25794969600 | bytes 52469760 | tf_op jit(solution)/shard_map/dot_general | solution.py:41
  138.8 3.0 slice_select_fusion.1
  141.9 104.4 %all-reduce.7.cloned.1.call-done = f32[4096,128]{1,0:T(8,128)} async-done(((f32[4096,128]{1,0:T(8,128)}), f32[4096,128]{1,0:T(8,128)}) %all-reduce.7.cloned.1.call-update) | async-done | bytes 2097168 | tf_op jit(solution)/shard_map/psum | solution.py:14
  246.3 1.5 slice_select_fusion.3
  248.1 31.2 %all-reduce.9.cloned.1.call-done = f32[128,128]{1,0:T(8,128)} async-done(((f32[128,128]{1,0:T(8,128)}), f32[128,128]{1,0:T(8,128)}) %all-reduce.9.cloned.1.call-update) | async-done | bytes 65552 | tf_op jit(solution)/shard_map/psum | solution.py:14
  279.3 0.9 copy.17
  280.2 0.9 fusion.25
  281.2 11.7 %cholesky.44 = f32[128,128]{1,0:T(8,128)S(1)} custom-call(f32[128,128]{1,0:T(8,128)S(1)} %copy.18), custom_call_target="Cholesky" | custom-call | tf_op jit(solution)/shard_map/jit(cholesky)/cholesky | solution.py:51
  293.6 0.7 select_bitcast_fusion.1
  294.2 9.8 %custom-call.6 = f32[1,128,128]{1,2,0:T(8,128)S(1)} custom-call(f32[1,128,128]{2,1,0:T(8,128)S(1)} %get-tuple-element.6), custom_call_target="InvertDiagBlocksLowerTriangular" | custom-call | tf_op jit(solution)/shard_map/jit(_solve_triangular)/triangular_solve | solution.py:52
  304.1 6.7 %fusion.35 = (bf16[4096,128]{1,0:T(8,128)(2,1)}, f32[4096,128]{1,0:T(8,128)S(1)}) fusion(f32[4096,128]{1,0:T(8,128)} %all-reduce.7.cloned.1.call-done, f32[1,128,128]{1,2,0:T(8,128)S(1)} %custom-call.6, f32[128,128]{1,0:T(8,128)S(1)} %get-tuple-element.7, pred[4096]{0:T(1024)(128)(4,1)S(1)} %get-tuple-element.12, pred[4096]{0:T(1024)(128)(4,1)S(1)} %get-tuple-element.13), kind=kOutput, calls=%fused_computation.63 | convolution fusion | flops 806879232 | bytes 5382144 | tf_op jit(solution)/shard_map/jit(_solve_triangular)/triangular_solve | solution.py:52
  311.1 35.7 %all-gather.7.cloned.1.call-done = bf16[16384,128]{1,0:T(8,128)(2,1)} async-done(((bf16[4096,128]{1,0:T(8,128)(2,1)}), bf16[16384,128]{1,0:T(8,128)(2,1)}) %all-gather.7.cloned.1.call-update) | async-done | bytes 4194320 | tf_op jit(solution)/shard_map/all_gather | solution.py:61
  346.8 31.7 %select_subtract_fusion.1 = f32[4096,2048]{1,0:T(8,128)} fusion(f32[4096,2048]{1,0:T(8,128)} %select_add_fusion, pred[2048]{0:T(1024)(128)(4,1)S(1)} %fusion.32, pred[4096]{0:T(1024)(128)(4,1)S(1)} %fusion.27, f32[4096,128]{1,0:T(8,128)S(1)} %get-tuple-element.9, bf16[16384,128]{1,0:T(8,128)(2,1)} %all-gather.7.cloned.1.call-done, s32[]{:T(128)S(6)} %select_n.63), kind=kOutput, calls=%fused_computation.1 | convolution fusion | flops 12910067712 | bytes 69736448 | tf_op jit(solution)/shard_map/dot_general | solution.py:65
  378.6 3.0 slice_select_fusion
  381.7 101.3 %all-reduce.11.cloned.1.call-done = f32[4096,128]{1,0:T(8,128)} async-done(((f32[4096,128]{1,0:T(8,128)}), f32[4096,128]{1,0:T(8,128)}) %all-reduce.11.cloned.1.call-update) | async-done | bytes 2097168 | tf_op jit(solution)/shard_map/psum | solution.py:14
  483.0 1.5 slice_select_fusion.2
  485.0 30.9 %all-reduce.13.cloned.1.call-done = f32[128,128]{1,0:T(8,128)} async-done(((f32[128,128]{1,0:T(8,128)}), f32[128,128]{1,0:T(8,128)}) %all-reduce.13.cloned.1.call-update) | async-done | bytes 65552 | tf_op jit(solution)/shard_map/psum | solution.py:14
  515.9 0.9 copy.20
  516.8 0.9 fusion.23
  517.8 11.7 %cholesky.55 = f32[128,128]{1,0:T(8,128)S(1)} custom-call(f32[128,128]{1,0:T(8,128)S(1)} %copy.21), custom_call_target="Cholesky" | custom-call | tf_op jit(solution)/shard_map/jit(cholesky)/cholesky | solution.py:51
  530.2 0.7 select_bitcast_fusion
  530.8 9.8 %custom-call.7 = f32[1,128,128]{1,2,0:T(8,128)S(1)} custom-call(f32[1,128,128]{2,1,0:T(8,128)S(1)} %get-tuple-element.4), custom_call_target="InvertDiagBlocksLowerTriangular" | custom-call | tf_op jit(solution)/shard_map/jit(_solve_triangular)/triangular_solve | solution.py:52
  540.7 7.3 %fusion.36 = (bf16[4096,128]{1,0:T(8,128)(2,1)}, f32[4096,128]{1,0:T(8,128)}) fusion(f32[4096,128]{1,0:T(8,128)} %all-reduce.11.cloned.1.call-done, f32[1,128,128]{1,2,0:T(8,128)S(1)} %custom-call.7, f32[128,128]{1,0:T(8,128)S(1)} %get-tuple-element.5, pred[4096]{0:T(1024)(128)(4,1)S(1)} %fusion.28, pred[4096]{0:T(1024)(128)(4,1)S(1)} %get-tuple-element.12), kind=kOutput, calls=%fused_computation.64 | convolution fusion | flops 806879232 | bytes 5382144 | tf_op jit(solution)/shard_map/jit(_solve_triangular)/triangular_solve | solution.py:52
  548.0 3.9 pad_maximum_fusion
  551.8 32.2 %all-gather.9.cloned.1.call-done = bf16[16384,128]{1,0:T(8,128)(2,1)} async-done(((bf16[4096,128]{1,0:T(8,128)(2,1)}), bf16[16384,128]{1,0:T(8,128)(2,1)}) %all-gather.9.cloned.1.call-update) | async-done | bytes 4194320 | tf_op jit(solution)/shard_map/all_gather | solution.py:61
  584.0 32.3 %select_subtract_fusion = f32[4096,2048]{1,0:T(8,128)} fusion(f32[4096,2048]{1,0:T(8,128)} %select_subtract_fusion.1, pred[2048]{0:T(1024)(128)(4,1)S(1)} %fusion.31, pred[4096]{0:T(1024)(128)(4,1)S(1)} %fusion.26, f32[4096,128]{1,0:T(8,128)} %get-tuple-element.11, bf16[16384,128]{1,0:T(8,128)(2,1)} %all-gather.9.cloned.1.call-done, s32[]{:T(128)S(6)} %select_n.63), kind=kOutput, calls=%fused_computation | convolution fusion | flops 12910067712 | bytes 69736448 | tf_op jit(solution)/shard_map/dot_general | solution.py:65
  (32 shorter events, 2.9 us)
Async XLA Ops:
  7.2 63.6 %all-gather.5.cloned.1.call-start = ((), (), s32[]{:S(2)}) async-start(), calls=%async_computation | async-start | bytes 3244032 | tf_op jit(solution)/shard_map/all_gather | solution.py:36
  7.9 238.4 %all-reduce.7.cloned.1.call-start = ((), (), s32[]{:S(2)}) async-start(), calls=%async_computation.1 | async-start | bytes 4194304 | tf_op jit(solution)/shard_map/psum | solution.py:14
  79.6 4.9 copy-start
  141.9 137.4 %all-reduce.9.cloned.1.call-start = ((), (), s32[]{:S(2)}) async-start(), calls=%async_computation.2 | async-start | bytes 131072 | tf_op jit(solution)/shard_map/psum | solution.py:14
  247.8 99.0 %all-gather.7.cloned.1.call-start = ((), (), s32[]{:S(2)}) async-start(), calls=%async_computation.3 | async-start | bytes 5242880 | tf_op jit(solution)/shard_map/all_gather | solution.py:61
  310.8 172.2 %all-reduce.11.cloned.1.call-start = ((), (), s32[]{:S(2)}) async-start(), calls=%async_computation.4 | async-start | bytes 4194304 | tf_op jit(solution)/shard_map/psum | solution.py:14
  381.6 134.3 %all-reduce.13.cloned.1.call-start = ((), (), s32[]{:S(2)}) async-start(), calls=%async_computation.5 | async-start | bytes 131072 | tf_op jit(solution)/shard_map/psum | solution.py:14
  484.4 99.5 %all-gather.9.cloned.1.call-start = ((), (), s32[]{:S(2)}) async-start(), calls=%async_computation.6 | async-start | bytes 5242880 | tf_op jit(solution)/shard_map/all_gather | solution.py:61
Sparse Core Ops, SparseCore 0:
  10.9 59.7 all-gather.4
  142.0 104.2 all-reduce.6
  249.2 30.0 all-reduce.8
  310.9 35.9 all-gather.6
  381.8 101.1 all-reduce.10
  485.8 30.0 all-reduce.12
  548.0 35.8 all-gather.8
where the time goes:
time: 629 us; the launch traced here: 623 us
  waiting for transfers between devices  341 us (54%)
  matrix products  143 us (23%)
  other arithmetic  60.4 us (10%)
  blocking collectives  58.6 us (9%)
  between operations  14.5 us (2%)
    psum x4, waiting for transfers between devices, spread_2(): return lax.psum(jnp.where(mine, x, jnp.zeros_like(x)), axis)  268 us
    all_gather x2, waiting for transfers between devices, shards(): lax.all_gather(panel_now.astype(jnp.bfloat16), 'row', axis=0, tiled=True)  67.9 us
    dot_general x2, matrix products, shards(): lax.dot_general(panel_now, across, (((1,), (1,)), ((), ())), precision=la...  64.1 us
    all_gather x1, blocking collectives, shards(): tile_part = lax.all_gather(tile_ids, ('row', 'col'), axis=0, tiled=True)  58.6 us
    dot_general x1, matrix products, shards(): lax.dot_general(row_side, col_side, (((0,), (0,)), ((), ())), preferred_e...  54.4 us
    another operation x6, other arithmetic, shards(): factor = jnp.linalg.cholesky(corner)  24.8 us
    another operation x4, other arithmetic, shards(): solved = jax.scipy.linalg.solve_triangular(factor, column.T, lower=True).T  20.9 us
    another operation x2, matrix products, shards(): solved = jax.scipy.linalg.solve_triangular(factor, column.T, lower=True).T  13.9 us
  transfers between devices with their start and end apart: 7, of which 7 were waited for; matrix products, arithmetic and copies ran while one was open for 1% of the time, Pallas kernels for 0%

commit v1 on v0

v1 whole, which is shorter than its diff:
```python
import functools

import jax
import jax.numpy as jnp
from jax import lax
from jax.experimental import pallas as pl
from jax.experimental.pallas import tpu as pltpu
from jax.sharding import PartitionSpec as P

TILE = 128
BT = 8
COLS = 16
PANEL = 128
PANELS = 2
WIDE = PANEL * PANELS
GROUP = 16
HIGH = lax.Precision.HIGHEST
MESH = pl.DeviceIdType.MESH


def gather_kernel(sizes, x_ref, s_ref, big_ref, small_ref, send_sem, recv_sem, own_sem):
    na, nb, nx, nc = sizes
    ncol = na * nb
    row_at, col_at = lax.axis_index("row"), lax.axis_index("col")
    a, b = col_at // nb, col_at % nb
    x, c = row_at // nc, row_at % nc

    def at(da, db, dx, dc):
        row = ((x + dx) % nx) * nc + (c + dc) % nc
        col = ((a + da) % na) * nb + (b + db) % nb
        return row, col

    def chunk(key):
        row, col = at(*key)
        return row * ncol + col

    def slot(key):
        return ((key[0] * nb + key[1]) * nx + key[2]) * nc + key[3]

    partners = [(d, 0, 0, 0) for d in range(1, na)]
    partners += [(0, d, 0, 0) for d in range(1, nb)]
    partners += [(0, 0, d, 0) for d in range(1, nx)]
    partners += [(0, 0, 0, d) for d in range(1, nc)]
    barrier = pltpu.get_barrier_semaphore()
    for p in partners:
        pl.semaphore_signal(barrier, inc=1, device_id=at(*p), device_id_type=MESH)
    pl.semaphore_wait(barrier, len(partners))

    own = (0, 0, 0, 0)
    keep = [
        pltpu.make_async_copy(x_ref, big_ref.at[chunk(own)], own_sem.at[0]),
        pltpu.make_async_copy(s_ref, small_ref.at[chunk(own)], own_sem.at[1]),
    ]
    started = []

    def send(key, axis):
        mine = chunk(key)
        for step in range(1, sizes[axis]):
            to = [0, 0, 0, 0]
            to[axis] = step
            there = list(key)
            there[axis] = (key[axis] - step) % sizes[axis]
            number = len(started)
            pairs = [
                (x_ref if key == own else big_ref.at[mine], big_ref.at[mine]),
                (s_ref if key == own else small_ref.at[mine], small_ref.at[mine]),
            ]
            for kind, (src, dst) in enumerate(pairs):
                copy = pltpu.make_async_remote_copy(
                    src_ref=src,
                    dst_ref=dst,
                    send_sem=send_sem.at[kind, number // 2],
                    recv_sem=recv_sem.at[kind, slot(there)],
                    device_id=at(*to),
                    device_id_type=MESH,
                )
                copy.start()
                started.append(copy)

    def arrive(key):
        mine = chunk(key)
        for kind, ref in enumerate((big_ref, small_ref)):
            pltpu.make_async_remote_copy(
                src_ref=ref.at[mine],
                dst_ref=ref.at[mine],
                send_sem=send_sem.at[kind, 0],
                recv_sem=recv_sem.at[kind, slot(key)],
                device_id=at(0, 0, 0, 1),
                device_id_type=MESH,
            ).wait_recv()

    send(own, 0)
    order = sorted(range(na), key=lambda d: min(d, na - d))
    first = {d: 1 if d % 2 == 0 else 2 for d in order}
    for d in order:
        key = (d, 0, 0, 0)
        if d:
            arrive(key)
        send(key, first[d])
        send(key, 3 - first[d])
        send(key, 3)
        if d == 0:
            for copy in keep:
                copy.start()
    for d in order:
        for step in range(1, sizes[first[d]]):
            key = [d, 0, 0, 0]
            key[first[d]] = step
            key = tuple(key)
            arrive(key)
            send(key, 3 - first[d])
            send(key, 3)
    for d in order:
        for step in range(1, sizes[3 - first[d]]):
            for before in range(sizes[first[d]]):
                key = [d, 0, 0, 0]
                key[first[d]] = before
                key[3 - first[d]] = step
                key = tuple(key)
                arrive(key)
                send(key, 3)
    for da in order:
        for db in range(nb):
            for dx in range(nx):
                arrive((da, db, dx, 1))
    for copy in started:
        copy.wait_send()
    for copy in keep:
        copy.wait()


def gather_all(x, small):
    nrow, ncol = lax.axis_size("row"), lax.axis_size("col")
    na = 4 if ncol % 4 == 0 else 1
    sizes = (na, ncol // na, nrow // 2, 2)
    count = nrow * ncol
    return pl.pallas_call(
        functools.partial(gather_kernel, sizes),
        out_shape=(
            jax.ShapeDtypeStruct((count,) + x.shape, x.dtype),
            jax.ShapeDtypeStruct((count,) + small.shape, small.dtype),
        ),
        in_specs=[pl.BlockSpec(memory_space=pl.ANY)] * 2,
        out_specs=(pl.BlockSpec(memory_space=pl.ANY),) * 2,
        scratch_shapes=[
            pltpu.SemaphoreType.DMA((2, count)),
            pltpu.SemaphoreType.DMA((2, count)),
            pltpu.SemaphoreType.DMA((2,)),
        ],
        compiler_params=pltpu.CompilerParams(collective_id=0, has_side_effects=True),
    )(x, small)


def assemble_kernel(
    comm, row_tiles, col_tiles, ids_ref, at_ref, blocks_ref, cols_ref, top_ref, edge_ref,
    bar_ref, rest_ref, panel_ref, left, right, lists, counts,
):
    step = pl.program_id(0)
    row_first, col_first = at_ref[0], at_ref[1]
    band = col_tiles * TILE

    @pl.when(step == 0)
    def _():
        left[...] = jnp.zeros_like(left)
        right[...] = jnp.zeros_like(right)

        def clear(i, _):
            counts[i] = 0
            return 0

        lax.fori_loop(0, row_tiles + 1, clear, 0)

        def enter(k, _):
            for s in range(BT):
                where = ids_ref[k * BT + s] - row_first
                inside = jnp.logical_and(where >= 0, where < row_tiles)
                where = jnp.where(inside, where, row_tiles)
                n = counts[where]
                lists[where * comm + jnp.minimum(n, comm - 1)] = k * BT + s
                counts[where] = n + 1
            return 0

        lax.fori_loop(0, comm, enter, 0)

    tile = row_first + step
    total = counts[step]

    def pick(chunk):
        base = chunk * GROUP
        some = jnp.minimum(total - base, GROUP)

        def one(j, _):
            entry = lists[step * comm + base + j]
            k, s = entry // BT, entry % BT
            src = pl.ds(pl.multiple_of(k * COLS, COLS), COLS)
            dst = pl.ds(pl.multiple_of(j * COLS, COLS), COLS)
            left[dst, :] = blocks_ref[src, pl.ds(pl.multiple_of(s * TILE, TILE), TILE)]
            right[dst, :] = cols_ref[src, :]
            return 0

        lax.fori_loop(0, some, one, 0)

        def blank(j, _):
            dst = pl.ds(pl.multiple_of(j * COLS, COLS), COLS)
            left[dst, :] = jnp.zeros((COLS, TILE), left.dtype)
            return 0

        lax.fori_loop(some, GROUP, blank, 0)

    def times():
        return lax.dot_general(
            left[...], right[...], (((0,), (0,)), ((), ())), preferred_element_type=jnp.float32
        )

    @pl.when(tile >= PANELS)
    def _():
        pick(0)
        got = times()
        rest_ref[...] = got[:, :band]
        panel_ref[...] = got[:, band : band + WIDE] + got[:, band + WIDE :]

        def more(chunk, _):
            pick(chunk)
            got = times()
            rest_ref[...] += got[:, :band]
            panel_ref[...] += got[:, band : band + WIDE] + got[:, band + WIDE :]
            return 0

        lax.fori_loop(1, (total + GROUP - 1) // GROUP, more, 0)

    @pl.when(tile < PANELS)
    def _():
        src = pl.ds(pl.multiple_of(jnp.minimum(tile, PANELS - 1) * TILE, TILE), TILE)
        rest_ref[...] = top_ref[src, :]
        panel_ref[...] = edge_ref[src, :]

    own = tile - col_first

    @pl.when(jnp.logical_and(own >= 0, own < col_tiles))
    def _():
        line = bar_ref[pl.ds(step, 1), :]
        there = lax.broadcasted_iota(jnp.int32, (TILE, TILE), 0)
        here = lax.broadcasted_iota(jnp.int32, (TILE, TILE), 1)
        spot = pl.ds(pl.multiple_of(own * TILE, TILE), TILE)
        rest_ref[:, spot] += jnp.where(there == here, jnp.broadcast_to(line, (TILE, TILE)), 0.0)


def assemble(ids, at, blocks, cols, top, edge, bar, row_tiles, col_tiles):
    comm = ids.shape[0] // BT
    band = col_tiles * TILE
    whole = pl.BlockSpec(memory_space=pltpu.VMEM)
    return pl.pallas_call(
        functools.partial(assemble_kernel, comm, row_tiles, col_tiles),
        grid_spec=pltpu.PrefetchScalarGridSpec(
            num_scalar_prefetch=2,
            grid=(row_tiles,),
            in_specs=[whole] * 5,
            out_specs=[
                pl.BlockSpec((TILE, band), lambda i, *_: (i, 0)),
                pl.BlockSpec((TILE, WIDE), lambda i, *_: (i, 0)),
            ],
            scratch_shapes=[
                pltpu.VMEM((GROUP * COLS, TILE), jnp.bfloat16),
                pltpu.VMEM((GROUP * COLS, cols.shape[1]), jnp.bfloat16),
                pltpu.SMEM(((row_tiles + 1) * comm,), jnp.int32),
                pltpu.SMEM((row_tiles + 1,), jnp.int32),
            ],
        ),
        out_shape=[
            jax.ShapeDtypeStruct((row_tiles * TILE, band), jnp.float32),
            jax.ShapeDtypeStruct((row_tiles * TILE, WIDE), jnp.float32),
        ],
        compiler_params=pltpu.CompilerParams(vmem_limit_bytes=48 * 1024 * 1024),
    )(ids, at, blocks, cols, top, edge, bar)


def expand(tiled, tile_list, first_tile, tile_count):
    wanted = first_tile + jnp.arange(tile_count, dtype=jnp.int32)
    onehot = (tile_list[:, :, None] == wanted[None, None, :]).astype(jnp.bfloat16)
    spread = jnp.einsum("kas,kjai->kjsi", onehot, tiled, preferred_element_type=jnp.float32)
    return spread.astype(jnp.bfloat16).reshape(
        tiled.shape[0] * tiled.shape[1], tile_count * tiled.shape[3]
    )


def mul(lhs, rhs, left, right, precision=HIGH):
    return lax.dot_general(
        lhs, rhs, (((left,), (right,)), ((), ())), precision=precision,
        preferred_element_type=jnp.float32,
    )


def split_two(v):
    hi = lax.reduce_precision(v, 8, 7)
    return hi.astype(jnp.bfloat16), (v - hi).astype(jnp.bfloat16)


def shards(blocks, tile_ids, barrier):
    nrow, ncol = lax.axis_size("row"), lax.axis_size("col")
    band_rows = barrier.shape[0]
    band_cols = band_rows * nrow // ncol
    row_tiles, col_tiles = band_rows // TILE, band_cols // TILE
    row_first = lax.axis_index("row") * row_tiles
    col_first = lax.axis_index("col") * col_tiles
    held = blocks.shape[0]
    depth = held * COLS
    spare = 8 * TILE - WIDE - held * BT
    small = jnp.concatenate(
        [barrier[:WIDE], tile_ids.reshape(-1).astype(jnp.float32), jnp.zeros((spare,), jnp.float32)]
    ).reshape(8, TILE)
    big, smalls = gather_all(blocks.reshape(depth, BT * TILE), small)
    smalls = smalls.reshape(smalls.shape[0], 8 * TILE)
    ids = smalls[:, WIDE : WIDE + held * BT].astype(jnp.int32).reshape(-1)
    top_bar = smalls[0, :WIDE]
    comm = ids.shape[0] // BT
    rows = big.reshape(comm * COLS, BT * TILE)
    tile_list = ids.reshape(comm, BT)
    tiled = rows.reshape(comm, COLS, BT, TILE)
    lead = expand(tiled, tile_list, 0, PANELS)
    cols = expand(tiled, tile_list, col_first, col_tiles)

    corner = mul(lead, lead, 0, 0, None) + jnp.diag(top_bar)
    eye = jnp.eye(PANEL, dtype=jnp.float32)
    f0 = jnp.linalg.cholesky(corner[:PANEL, :PANEL])
    w0 = jax.scipy.linalg.solve_triangular(f0, eye, lower=True)
    x10 = mul(corner[PANEL:, :PANEL], w0, 1, 1)
    f1 = jnp.linalg.cholesky(corner[PANEL:, PANEL:] - mul(x10, x10, 1, 1))
    w1 = jax.scipy.linalg.solve_triangular(f1, eye, lower=True)
    edge = jnp.concatenate(
        [
            jnp.concatenate([f0, jnp.zeros_like(f0)], axis=1),
            jnp.concatenate([x10, f1], axis=1),
        ],
        axis=0,
    )
    inv = jnp.concatenate(
        [
            jnp.concatenate([w0, jnp.zeros_like(w0)], axis=1),
            jnp.concatenate([-mul(mul(w1, x10, 1, 0), w0, 1, 0), w1], axis=1),
        ],
        axis=0,
    )
    i_hi, i_lo = split_two(inv)
    q = mul(lead, i_hi, 1, 1, None) + mul(lead, i_lo, 1, 1, None)
    q_hi, q_lo = split_two(q)
    t = mul(q_hi, cols, 0, 0, None) + mul(q_lo, cols, 0, 0, None)
    col_tile = col_first + jnp.arange(band_cols, dtype=jnp.int32)[None, :] // TILE
    done = jnp.arange(WIDE, dtype=jnp.int32)[:, None] // PANEL < col_tile
    t = jnp.where(done, t, 0.0)
    t_hi, t_lo = split_two(t)
    away = mul(q_hi, t_hi, 1, 0, None) + mul(q_hi, t_lo, 1, 0, None) + mul(q_lo, t_hi, 1, 0, None)
    rhs = jnp.concatenate(
        [(cols.astype(jnp.float32) - away).astype(jnp.bfloat16), q_hi, q_lo], axis=1
    )
    top = mul(lead, cols, 0, 0, None)
    lower = mul(x10, t[:PANEL], 1, 0)
    top = top - jnp.concatenate([jnp.zeros_like(lower), lower], axis=0)
    at = jnp.stack([row_first, col_first]).astype(jnp.int32)
    rest, panels = assemble(
        ids, at, rows, rhs, top, edge, barrier.reshape(row_tiles, TILE), row_tiles, col_tiles
    )
    return panels, rest


def solution(mesh):
    placed = (P(("row", "col"), None, None), P(("row", "col"), None), P("row"))
    return jax.shard_map(
        shards,
        mesh=mesh,
        in_specs=placed,
        out_specs=(P("row", None), P("row", "col")),
        check_vma=False,
    )
```

time: 629 us -> 186 us (0.30)
  waiting for transfers between devices: 341 us -> 0 us
  matrix products: 143 us -> 50.3 us
  Pallas kernels: 0 us -> 66.3 us
  blocking collectives: 58.6 us -> 0 us
  between operations: 14.5 us -> 0.94 us
    psum x4 -> x0, waiting for transfers between devices: 268 us -> none  [spread_2(): return lax.psum(jnp.where(mine, x, jnp.zeros_like(x)), axis)]
    dot_general x3 -> x14, matrix products: 118 us -> 43 us  [mul(): lax.dot_general(lhs, rhs, (((left,), (right,)), ((), ())), precision=prec...]
    all_gather x3 -> x0, waiting for transfers between devices: 72 us -> none  [the longest x2 67.9 us: shards(): lax.all_gather(panel_now.astype(jnp.bfloat16), 'row', axis=0, tiled=True)]
    pallas_call x0 -> x2, Pallas kernels: none -> 66.3 us  [the longest x1 36.1 us: assemble(): pl.pallas_call(functools.partial(assemble_kernel, comm, row_tiles, col_ti...]
    all_gather x1 -> x0, blocking collectives: 58.6 us -> none  [shards(): tile_part = lax.all_gather(tile_ids, ('row', 'col'), axis=0, tiled=True)]
    another operation x2, matrix products: 13.9 us -> 0.55 us  [the longest x1 0.28 us: shards(): w0 = jax.scipy.linalg.solve_triangular(f0, eye, lower=True)]
    select_n x4 -> x1, other arithmetic: 9.04 us -> 0.59 us  [shards(): done = jnp.arange(WIDE, dtype=jnp.int32)[:, None] // PANEL < col_tile]
    another operation x10 -> x11, other arithmetic: 45.7 us -> 48.9 us  [the longest x3 13.3 us: shards(): f0 = jnp.linalg.cholesky(corner[:PANEL, :PANEL])]
  transfers between devices with their start and end apart: 7 -> 0, of which waited for: 7 -> 0; matrix products, arithmetic and copies ran while one was open for 1% -> 0% of each run, Pallas kernels for 0% -> 0%
where the time goes in v1:
time: 186 us
  Pallas kernels  66.3 us (36%)
  other arithmetic  60 us (32%)
  matrix products  50.3 us (27%)
  local copies, waits for them, and re-layouts  8.67 us (5%)
    dot_general x14, matrix products, mul(): lax.dot_general(lhs, rhs, (((left,), (right,)), ((), ())), precision=prec...  43 us
    pallas_call x1, Pallas kernels, assemble(): pl.pallas_call(functools.partial(assemble_kernel, comm, row_tiles, col_ti...  36.1 us
    pallas_call x1, Pallas kernels, gather_all(): pl.pallas_call(functools.partial(gather_kernel, sizes), out_shape=(jax.Sh...  30.2 us
    another operation x3, other arithmetic, shards(): f0 = jnp.linalg.cholesky(corner[:PANEL, :PANEL])  13.3 us
    another operation x3, other arithmetic, shards(): f1 = jnp.linalg.cholesky(corner[PANEL:, PANEL:] - mul(x10, x10, 1, 1))  12.5 us
    another operation x2, other arithmetic, shards(): w0 = jax.scipy.linalg.solve_triangular(f0, eye, lower=True)  11.9 us
    another operation x2, other arithmetic, shards(): w1 = jax.scipy.linalg.solve_triangular(f1, eye, lower=True)  11.1 us
    concatenate x1, other arithmetic, shards(): jnp.concatenate([(cols.astype(jnp.float32) - away).astype(jnp.bfloat16),...  7.06 us

profile of v1, /device:TPU:9, one launch (start us, length us, event | category | flops | bytes accessed | tf_op | source)
XLA Modules:
  0.0 186.3 jit_solution(13233125739456258500)
XLA Ops:
  1.2 0.7 slice.29
  2.5 0.7 convert_element_type.52
  4.0 30.2 %shard_map.50 = (bf16[32,48,1024]{2,1,0:T(8,128)(2,1)}, f32[32,8,128]{2,1,0:T(8,128)}) custom-call(bf16[48,1024]{1,0:T(8,128)(2,1)} %bitcast.114, f32[8,128]{1,0:T(8,128)} %maximum_bitcast_fusion.s_ref), custom_call_target="tpu_custom_call" | custom-call | tf_op jit(solution)/shard_map/pallas_call | solution.py:137
  34.2 0.9 copy.72
  35.3 2.7 %copy.31 = bf16[192,8,8,128]{3,2,1,0:T(8,128)(2,1)S(1)} copy(bf16[192,8,8,128]{3,1,2,0:T(8,128)(2,1)} %bitcast.98) | data formatting | bytes 6291456
  38.1 1.0 fusion.23
  39.0 0.9 copy-done.6
  41.0 0.9 copy.15
  42.6 12.5 %cholesky.44 = f32[128,128]{1,0:T(8,128)S(1)} custom-call(f32[128,128]{1,0:T(8,128)} %fusion.62), custom_call_target="Cholesky" | custom-call | tf_op jit(solution)/shard_map/jit(cholesky)/cholesky | solution.py:324
  55.9 1.3 select_bitcast_fusion.1
  57.2 10.6 %custom-call.6 = f32[1,128,128]{1,2,0:T(8,128)S(1)} custom-call(f32[1,128,128]{2,1,0:T(8,128)} %get-tuple-element.14), custom_call_target="InvertDiagBlocksLowerTriangular" | custom-call | tf_op jit(solution)/shard_map/jit(_solve_triangular)/triangular_solve | solution.py:325
  68.1 1.0 fusion.57
  69.2 1.1 convolution_subtract_fusion
  70.4 11.8 %cholesky.55 = f32[128,128]{1,0:T(8,128)S(1)} custom-call(f32[128,128]{1,0:T(8,128)S(1)} %fusion.60), custom_call_target="Cholesky" | custom-call | tf_op jit(solution)/shard_map/jit(cholesky)/cholesky | solution.py:327
  83.0 1.3 select_bitcast_fusion
  84.3 9.8 %custom-call.7 = f32[1,128,128]{1,2,0:T(8,128)S(1)} custom-call(f32[1,128,128]{2,1,0:T(8,128)S(1)} %get-tuple-element.12), custom_call_target="InvertDiagBlocksLowerTriangular" | custom-call | tf_op jit(solution)/shard_map/jit(_solve_triangular)/triangular_solve | solution.py:328
  94.3 0.7 copy.19
  95.4 0.8 convolution_negate_fusion
  96.2 0.7 copy.22
  96.9 0.9 select_maximum_fusion.edge_ref
  97.8 1.5 fusion.32
  99.4 1.6 reduce-precision_convert_fusion.1
  101.0 5.8 %convolution_convert_fusion = bf16[96,16,128,16]{2,3,1,0:T(8,128)(2,1)S(1)} fusion(s32[16]{0:T(128)} %iota_add_fusion, s32[96,8]{1,0:T(8,128)S(1)} %copy-done.10, bf16[96,16,8,128]{3,2,1,0:T(8,128)(2,1)S(1)} %bitcast.102), kind=kOutput, calls=%fused_computation.11 | convolution fusion | flops 53489664 | bytes 9440320 | tf_op jit(solution)/shard_map/kas,kjai->kjsi/dot_general | solution.py:280
  106.8 1.8 fusion.2
  108.6 1.9 fusion.18
  110.5 1.3 fusion.28
  111.8 1.8 fusion.15.top_ref
  113.7 6.4 %fusion.26 = f32[1536,2048]{1,0:T(8,128)} fusion(bf16[1536,256]{1,0:T(8,128)(2,1)S(1)} %get-tuple-element.16, f32[256,2048]{1,0:T(8,128)S(1)} %fusion.18), kind=kOutput, calls=%fused_computation.29 | convolution fusion | flops 1612185600 | bytes 15466496 | tf_op jit(solution)/shard_map/dot_general | solution.py:287
  120.1 6.6 %fusion.39 = f32[1536,2048]{1,0:T(8,128)} fusion(bf16[1536,256]{1,0:T(8,128)(2,1)S(1)} %get-tuple-element.16, f32[256,2048]{1,0:T(8,128)S(1)} %fusion.18), kind=kOutput, calls=%fused_computation.41 | convolution fusion | flops 1611661312 | bytes 15466496 | tf_op jit(solution)/shard_map/dot_general | solution.py:287
  126.6 16.5 %subtract_convert_fusion = bf16[1536,2048]{1,0:T(8,128)(2,1)} fusion(f32[1536,2048]{1,0:T(8,128)} %fusion.39, f32[1536,2048]{1,0:T(8,128)} %fusion.26, bf16[1536,256]{1,0:T(8,128)(2,1)} %copy-done.8, bf16[192,8,16,128]{3,2,1,0:T(8,128)(2,1)} %bitcast.106, f32[256,2048]{1,0:T(8,128)} %copy-done.2), kind=kOutput, calls=%fused_computation | convolution fusion | flops 1627389952 | bytes 40632320 | tf_op jit(solution)/shard_map/dot_general | solution.py:287
  143.1 7.1 %pad_maximum_fusion.cols_ref = bf16[1536,2560]{1,0:T(8,128)(2,1)} fusion(bf16[1536,256]{1,0:T(8,128)(2,1)} %copy-done.8, bf16[1536,256]{1,0:T(8,128)(2,1)S(1)} %copy-done.5, bf16[1536,2048]{1,0:T(8,128)(2,1)} %subtract_convert_fusion), kind=kLoop, calls=%fused_computation.1 | loop fusion | flops 23592960 | bytes 15728640 | tf_op jit(solution)/shard_map/concatenate | solution.py:352
  150.2 36.1 %shard_map.51 = (f32[4096,2048]{1,0:T(8,128)}, f32[4096,256]{1,0:T(8,128)}) custom-call(s32[768]{0:T(1024)S(1)} %reshape.124.ids_ref, s32[2]{0:T(128)S(1)} %pad_add_fusion.at_ref, bf16[1536,1024]{1,0:T(8,128)(2,1)S(1)} %bitcast.99, bf16[1536,2560]{1,0:T(8,128)(2,1)} %pad_maximum_fusion.cols_ref, f32[256,2048]{1,0:T(8,128)S(1)} %fusion.15.top_ref, ...), custom_call_target="tpu_custom_call" | custom-call | tf_op jit(solution)/shard_map/pallas_call | solution.py:252
  (48 shorter events, 6.3 us)
Async XLA Ops:
  35.3 7.3 %copy-start.9 = (s32[96,8]{1,0:T(8,128)}, s32[96,8]{1,0:T(8,128)S(1)}, u32[]{:S(2)}) copy-start(s32[96,8]{1,0:T(8,128)S(1)} %eq.37) | copy-start | bytes 9220
  39.0 0.9 copy-start.6
  40.4 16.8 %copy-start.11 = (f32[256,256]{0,1:T(8,128)}, f32[256,256]{0,1:T(8,128)S(1)}, u32[]{:S(2)}) copy-start(f32[256,256]{0,1:T(8,128)S(1)} %convolution_add_fusion.1) | copy-start | bytes 786436
  96.9 4.1 %copy-start.10 = (s32[96,8]{1,0:T(8,128)S(1)}, s32[96,8]{1,0:T(8,128)}, u32[]{:S(2)}) copy-start(s32[96,8]{1,0:T(8,128)} %copy-done.9) | copy-start | bytes 9220
  101.0 7.6 %copy-start.8 = (bf16[1536,256]{1,0:T(8,128)(2,1)}, bf16[1536,256]{1,0:T(8,128)(2,1)S(1)}, u32[]{:S(2)}) copy-start(bf16[1536,256]{1,0:T(8,128)(2,1)S(1)} %get-tuple-element.17) | copy-start | bytes 2359300
  101.0 19.1 %copy-start.4 = (bf16[1536,256]{1,0:T(8,128)(2,1)}, bf16[1536,256]{1,0:T(8,128)(2,1)S(1)}, u32[]{:S(2)}) copy-start(bf16[1536,256]{1,0:T(8,128)(2,1)S(1)} %get-tuple-element.16) | copy-start | bytes 2359300
  106.8 5.1 %copy-start.3 = (bf16[96,16,128,16]{2,3,1,0:T(8,128)(2,1)}, bf16[96,16,128,16]{2,3,1,0:T(8,128)(2,1)S(1)}, u32[]{:S(2)}) copy-start(bf16[96,16,128,16]{2,3,1,0:T(8,128)(2,1)S(1)} %convolution_convert_fusion) | copy-start | bytes 18874372
  106.8 1.8 copy-start.12
  108.6 3.2 %copy-start.7 = (bf16[96,16,128,2]{2,3,1,0:T(2,128)(2,1)S(1)}, bf16[96,16,128,2]{2,3,1,0:T(2,128)(2,1)}, u32[]{:S(2)}) copy-start(bf16[96,16,128,2]{2,3,1,0:T(2,128)(2,1)} %copy-done.6) | copy-start | bytes 2359300
  110.5 9.5 %copy-start.2 = (f32[256,2048]{1,0:T(8,128)}, f32[256,2048]{1,0:T(8,128)S(1)}, u32[]{:S(2)}) copy-start(f32[256,2048]{1,0:T(8,128)S(1)} %fusion.18) | copy-start | bytes 6291460
  126.6 16.5 %copy-start.5 = (bf16[1536,256]{1,0:T(8,128)(2,1)S(1)}, bf16[1536,256]{1,0:T(8,128)(2,1)}, u32[]{:S(2)}) copy-start(bf16[1536,256]{1,0:T(8,128)(2,1)} %copy-done.4) | copy-start | bytes 2359300
  143.1 7.1 %copy-start = (bf16[32,48,1024]{2,1,0:T(8,128)(2,1)S(1)}, bf16[32,48,1024]{2,1,0:T(8,128)(2,1)}, u32[]{:S(2)}) copy-start(bf16[32,48,1024]{2,1,0:T(8,128)(2,1)} %get-tuple-element.9) | copy-start | bytes 9437188
  143.1 7.1 %copy-start.1 = (f32[4096]{0:T(1024)S(1)}, f32[4096]{0:T(1024)}, u32[]{:S(2)}) copy-start(f32[4096]{0:T(1024)} %param.8) | copy-start | bytes 49156

commit v2 on v1

--- a/solution.py
+++ b/solution.py
@@ -152,7 +152,7 @@
 
 
 def assemble_kernel(
-    comm, row_tiles, col_tiles, ids_ref, at_ref, blocks_ref, cols_ref, top_ref, edge_ref,
+    comm, row_tiles, col_tiles, ids_ref, at_ref, blocks_ref, cols_ref, q_ref, top_ref, edge_ref,
     bar_ref, rest_ref, panel_ref, left, right, lists, counts,
 ):
     step = pl.program_id(0)
@@ -195,7 +195,8 @@
             src = pl.ds(pl.multiple_of(k * COLS, COLS), COLS)
             dst = pl.ds(pl.multiple_of(j * COLS, COLS), COLS)
             left[dst, :] = blocks_ref[src, pl.ds(pl.multiple_of(s * TILE, TILE), TILE)]
-            right[dst, :] = cols_ref[src, :]
+            right[dst, :band] = cols_ref[src, :]
+            right[dst, band:] = q_ref[src, :]
             return 0
 
         lax.fori_loop(0, some, one, 0)
@@ -245,7 +246,7 @@
         rest_ref[:, spot] += jnp.where(there == here, jnp.broadcast_to(line, (TILE, TILE)), 0.0)
 
 
-def assemble(ids, at, blocks, cols, top, edge, bar, row_tiles, col_tiles):
+def assemble(ids, at, blocks, cols, q, top, edge, bar, row_tiles, col_tiles):
     comm = ids.shape[0] // BT
     band = col_tiles * TILE
     whole = pl.BlockSpec(memory_space=pltpu.VMEM)
@@ -254,14 +255,14 @@
         grid_spec=pltpu.PrefetchScalarGridSpec(
             num_scalar_prefetch=2,
             grid=(row_tiles,),
-            in_specs=[whole] * 5,
+            in_specs=[whole] * 6,
             out_specs=[
                 pl.BlockSpec((TILE, band), lambda i, *_: (i, 0)),
                 pl.BlockSpec((TILE, WIDE), lambda i, *_: (i, 0)),
             ],
             scratch_shapes=[
                 pltpu.VMEM((GROUP * COLS, TILE), jnp.bfloat16),
-                pltpu.VMEM((GROUP * COLS, cols.shape[1]), jnp.bfloat16),
+                pltpu.VMEM((GROUP * COLS, band + q.shape[1]), jnp.bfloat16),
                 pltpu.SMEM(((row_tiles + 1) * comm,), jnp.int32),
                 pltpu.SMEM((row_tiles + 1,), jnp.int32),
             ],
@@ -271,7 +272,61 @@
             jax.ShapeDtypeStruct((row_tiles * TILE, WIDE), jnp.float32),
         ],
         compiler_params=pltpu.CompilerParams(vmem_limit_bytes=48 * 1024 * 1024),
-    )(ids, at, blocks, cols, top, edge, bar)
+    )(ids, at, blocks, cols, q, top, edge, bar)
+
+
+def factor_kernel(corner_ref, edge_ref, inv_ref, work):
+    size = corner_ref.shape[0]
+    work[:, :size] = corner_ref[...]
+    there = lax.broadcasted_iota(jnp.int32, (size, size), 0)
+    here = lax.broadcasted_iota(jnp.int32, (size, size), 1)
+    work[:, size:] = jnp.where(there == here, 1.0, 0.0)
+    sub = lax.broadcasted_iota(jnp.int32, (8, 1), 0)
+    lane = lax.broadcasted_iota(jnp.int32, (8, TILE), 1)
+    wide = lax.broadcasted_iota(jnp.int32, (8, size), 1)
+    for first in range(0, size, 8):
+        low = first // TILE * TILE
+        high = low + TILE
+        panel = work[first : first + 8, low : size + high]
+        slab = panel[:, :TILE]
+        line = [
+            jnp.sum(jnp.where(lane == first - low + c, slab, 0.0), axis=1, keepdims=True)
+            for c in range(8)
+        ]
+        for j in range(8):
+            scale = lax.rsqrt(line[j][j : j + 1, :])
+            drop = jnp.where(sub > j, line[j] * scale, 0.0)
+            now = panel[j : j + 1, :] * scale
+            panel = jnp.where(sub == j, now, panel - drop * now)
+            for c in range(j + 1, 8):
+                line[c] = line[c] - drop * (line[c][j : j + 1, :] * scale)
+        upper = jnp.where(wide[:, low:] >= sub + first, panel[:, : size - low], 0.0)
+        work[first : first + 8, low:size] = upper
+        if low:
+            work[first : first + 8, :low] = jnp.zeros((8, low), jnp.float32)
+        inv_ref[first : first + 8, :high] = panel[:, size - low :]
+        if high < size:
+            inv_ref[first : first + 8, high:] = jnp.zeros((8, size - high), jnp.float32)
+        after = first + 8
+        if after < size:
+            left = jnp.where(wide[:, low:] >= after, upper, 0.0)
+            work[low:, low : size + high] -= lax.dot_general(
+                left, panel, (((0,), (0,)), ((), ())), precision=HIGH,
+                preferred_element_type=jnp.float32,
+            )
+    edge_ref[...] = work[:, :size].T
+
+
+def factor(corner):
+    spec = pl.BlockSpec(memory_space=pltpu.VMEM)
+    size = corner.shape[0]
+    return pl.pallas_call(
+        factor_kernel,
+        out_shape=[jax.ShapeDtypeStruct(corner.shape, jnp.float32)] * 2,
+        in_specs=[spec],
+        out_specs=[spec, spec],
+        scratch_shapes=[pltpu.VMEM((size, 2 * size), jnp.float32)],
+    )(corner)
 
 
 def expand(tiled, tile_list, first_tile, tile_count):
@@ -320,44 +375,24 @@
     cols = expand(tiled, tile_list, col_first, col_tiles)
 
     corner = mul(lead, lead, 0, 0, None) + jnp.diag(top_bar)
-    eye = jnp.eye(PANEL, dtype=jnp.float32)
-    f0 = jnp.linalg.cholesky(corner[:PANEL, :PANEL])
-    w0 = jax.scipy.linalg.solve_triangular(f0, eye, lower=True)
-    x10 = mul(corner[PANEL:, :PANEL], w0, 1, 1)
-    f1 = jnp.linalg.cholesky(corner[PANEL:, PANEL:] - mul(x10, x10, 1, 1))
-    w1 = jax.scipy.linalg.solve_triangular(f1, eye, lower=True)
-    edge = jnp.concatenate(
-        [
-            jnp.concatenate([f0, jnp.zeros_like(f0)], axis=1),
-            jnp.concatenate([x10, f1], axis=1),
-        ],
-        axis=0,
-    )
-    inv = jnp.concatenate(
-        [
-            jnp.concatenate([w0, jnp.zeros_like(w0)], axis=1),
-            jnp.concatenate([-mul(mul(w1, x10, 1, 0), w0, 1, 0), w1], axis=1),
-        ],
-        axis=0,
-    )
+    edge, inv = factor(corner)
+    x10 = edge[PANEL:, :PANEL]
     i_hi, i_lo = split_two(inv)
     q = mul(lead, i_hi, 1, 1, None) + mul(lead, i_lo, 1, 1, None)
     q_hi, q_lo = split_two(q)
-    t = mul(q_hi, cols, 0, 0, None) + mul(q_lo, cols, 0, 0, None)
+    t = mul(q_hi, cols, 0, 0, None)
     col_tile = col_first + jnp.arange(band_cols, dtype=jnp.int32)[None, :] // TILE
     done = jnp.arange(WIDE, dtype=jnp.int32)[:, None] // PANEL < col_tile
     t = jnp.where(done, t, 0.0)
-    t_hi, t_lo = split_two(t)
-    away = mul(q_hi, t_hi, 1, 0, None) + mul(q_hi, t_lo, 1, 0, None) + mul(q_lo, t_hi, 1, 0, None)
-    rhs = jnp.concatenate(
-        [(cols.astype(jnp.float32) - away).astype(jnp.bfloat16), q_hi, q_lo], axis=1
-    )
+    away = mul(q_hi, t.astype(jnp.bfloat16), 1, 0, None)
+    rhs = (cols.astype(jnp.float32) - away).astype(jnp.bfloat16)
+    qs = jnp.concatenate([q_hi, q_lo], axis=1)
     top = mul(lead, cols, 0, 0, None)
     lower = mul(x10, t[:PANEL], 1, 0)
     top = top - jnp.concatenate([jnp.zeros_like(lower), lower], axis=0)
     at = jnp.stack([row_first, col_first]).astype(jnp.int32)
     rest, panels = assemble(
-        ids, at, rows, rhs, top, edge, barrier.reshape(row_tiles, TILE), row_tiles, col_tiles
+        ids, at, rows, rhs, qs, top, edge, barrier.reshape(row_tiles, TILE), row_tiles, col_tiles
     )
     return panels, rest
 

time: 186 us -> 116 us (0.62)
  other arithmetic: 60 us -> 1.57 us
  matrix products: 50.3 us -> 20.8 us
  Pallas kernels: 66.3 us -> 86.3 us
  local copies, waits for them, and re-layouts: 8.67 us -> 5.46 us
    another operation x10 -> x0, other arithmetic: 48.8 us -> none  [the longest x3 13.3 us: shards(): f0 = jnp.linalg.cholesky(corner[:PANEL, :PANEL])]
    dot_general x14 -> x7, matrix products: 43 us -> 14.6 us  [mul(): lax.dot_general(lhs, rhs, (((left,), (right,)), ((), ())), precision=prec...]
    pallas_call x0 -> x1, Pallas kernels: none -> 21.6 us  [factor(): pl.pallas_call(factor_kernel, out_shape=[jax.ShapeDtypeStruct(corner.shap...]
    concatenate x2 -> x1, other arithmetic: 7.99 us -> 0.12 us  [shards(): qs = jnp.concatenate([q_hi, q_lo], axis=1)]
    unnamed x28 -> x10, local copies, waits for them, and re-layouts: 4.58 us -> 4.52 us
where the time goes in v2:
time: 116 us; the launch traced here: 115 us
  Pallas kernels  86.3 us (74%)
  matrix products  20.8 us (18%)
  local copies, waits for them, and re-layouts  5.46 us (5%)
  other arithmetic  1.57 us (1%)
    pallas_call x1, Pallas kernels, assemble(): pl.pallas_call(functools.partial(assemble_kernel, comm, row_tiles, col_ti...  34.4 us
    pallas_call x1, Pallas kernels, gather_all(): pl.pallas_call(functools.partial(gather_kernel, sizes), out_shape=(jax.Sh...  30.2 us
    pallas_call x1, Pallas kernels, factor(): pl.pallas_call(factor_kernel, out_shape=[jax.ShapeDtypeStruct(corner.shap...  21.6 us
    dot_general x7, matrix products, mul(): lax.dot_general(lhs, rhs, (((left,), (right,)), ((), ())), precision=prec...  14.6 us
    dot_general x2, matrix products, expand(): jnp.einsum('kas,kjai->kjsi', onehot, tiled, preferred_element_type=jnp.fl...  6.18 us
    unnamed x10, local copies, waits for them, and re-layouts  4.52 us

profile of v2, /device:TPU:9, one launch (start us, length us, event | category | flops | bytes accessed | tf_op | source)
XLA Modules:
  0.0 114.8 jit_solution(14708487788651060775)
XLA Ops:
  0.6 0.1 pad_add_fusion.at_ref
  0.7 0.7 slice.15
  1.4 0.7 convert_element_type.44
  2.1 0.1 convert_element_type.45
  2.2 0.7 maximum_bitcast_fusion.s_ref
  2.9 30.2 %shard_map.50 = (bf16[32,48,1024]{2,1,0:T(8,128)(2,1)}, f32[32,8,128]{2,1,0:T(8,128)}) custom-call(bf16[48,1024]{1,0:T(8,128)(2,1)} %bitcast.80, f32[8,128]{1,0:T(8,128)} %maximum_bitcast_fusion.s_ref), custom_call_target="tpu_custom_call" | custom-call | tf_op jit(solution)/shard_map/pallas_call | solution.py:137
  33.1 0.9 copy.49
  34.1 0.1 reshape.116.ids_ref
  34.1 0.1 eq.32
  34.2 2.7 %copy.14 = bf16[192,8,8,128]{3,2,1,0:T(8,128)(2,1)S(1)} copy(bf16[192,8,8,128]{3,1,2,0:T(8,128)(2,1)} %bitcast.71) | data formatting | bytes 6291456
  36.9 1.0 fusion.16
  37.9 0.0 copy-start.2
  38.0 0.9 copy-done.2
  38.8 1.1 convolution_add_fusion.1.corner_ref
  39.9 21.6 %shard_map.51 = (f32[256,256]{1,0:T(8,128)}, f32[256,256]{1,0:T(8,128)}) custom-call(f32[256,256]{1,0:T(8,128)} %convolution_add_fusion.1.corner_ref), custom_call_target="tpu_custom_call" | custom-call | tf_op jit(solution)/shard_map/pallas_call | solution.py:323
  61.5 0.0 copy-start.3
  61.5 1.7 %fusion.24 = f32[1536,256]{1,0:T(8,128)S(1)} fusion(bf16[192,8,2,128]{3,2,1,0:T(2,128)(2,1)} %bitcast.74, f32[256,256]{1,0:T(8,128)} %get-tuple-element.10), kind=kOutput, calls=%fused_computation.25 | convolution fusion | flops 201457664 | bytes 2621440 | tf_op jit(solution)/shard_map/dot_general | solution.py:342
  63.2 0.0 copy-done.3
  63.2 1.4 %fusion.15 = (bf16[1536,256]{1,0:T(8,128)(2,1)S(1)}, bf16[1536,256]{1,0:T(8,128)(2,1)S(1)}) fusion(f32[1536,256]{1,0:T(8,128)S(1)} %fusion.24, f32[256,256]{1,0:T(8,128)} %get-tuple-element.10, bf16[192,8,2,128]{3,2,1,0:T(2,128)(2,1)S(1)} %bitcast.75), kind=kOutput, calls=%fused_computation.16 | convolution fusion | flops 203489280 | bytes 4194304 | tf_op jit(solution)/shard_map/dot_general | solution.py:342
  64.6 0.1 pad_maximum_fusion.q_ref
  64.7 5.2 %convolution_convert_fusion = bf16[96,16,128,16]{2,3,1,0:T(8,128)(2,1)S(1)} fusion(s32[16]{0:T(128)S(1)} %iota_add_fusion, s32[96,8]{1,0:T(8,128)S(1)} %eq.32, bf16[96,16,8,128]{3,2,1,0:T(8,128)(2,1)S(1)} %bitcast.70), kind=kOutput, calls=%fused_computation.7 | convolution fusion | flops 53489664 | bytes 9440320 | tf_op jit(solution)/shard_map/kas,kjai->kjsi/dot_general | solution.py:335
  69.9 0.0 copy-start
  69.9 1.8 %fusion.12 = f32[256,2048]{1,0:T(8,128)S(1)} fusion(bf16[1536,256]{1,0:T(8,128)(2,1)S(1)} %get-tuple-element.15, bf16[192,8,16,128]{3,2,1,0:T(8,128)(2,1)S(1)} %bitcast.66, s32[2048]{0:T(1024)S(1)} %fusion.42, s32[256]{0:T(256)S(1)} %and_select_fusion), kind=kOutput, calls=%fused_computation.13 | convolution fusion | flops 1611661312 | bytes 9184256 | tf_op jit(solution)/shard_map/dot_general | solution.py:342
  71.7 0.0 copy-done
  71.7 1.0 fusion.19
  72.8 1.8 %fusion.9.top_ref = f32[256,2048]{1,0:T(8,128)S(1)} fusion(bf16[192,8,16,128]{3,2,1,0:T(8,128)(2,1)S(1)} %bitcast.67, f32[128,2048]{1,0:T(8,128)S(1)} %fusion.19, bf16[192,8,2,128]{3,2,1,0:T(2,128)(2,1)S(1)} %bitcast.76), kind=kOutput, calls=%fused_computation.12 | convolution fusion | flops 1611137024 | bytes 10223616 | tf_op jit(solution)/shard_map/dot_general | solution.py:342
  74.6 0.0 copy-start.1
  74.6 5.8 %subtract_convert_fusion.cols_ref = bf16[1536,2048]{1,0:T(8,128)(2,1)} fusion(bf16[1536,256]{1,0:T(8,128)(2,1)S(1)} %get-tuple-element.15, bf16[192,8,16,128]{3,2,1,0:T(8,128)(2,1)S(1)} %bitcast.68, f32[256,2048]{1,0:T(8,128)S(1)} %fusion.12), kind=kOutput, calls=%fused_computation | convolution fusion | flops 1620574208 | bytes 15466496 | tf_op jit(solution)/shard_map/dot_general | solution.py:342
  80.4 0.0 copy-done.1
  80.4 34.4 %shard_map.52 = (f32[4096,2048]{1,0:T(8,128)}, f32[4096,256]{1,0:T(8,128)}) custom-call(s32[768]{0:T(1024)S(1)} %reshape.116.ids_ref, s32[2]{0:T(128)S(1)} %pad_add_fusion.at_ref, bf16[1536,1024]{1,0:T(8,128)(2,1)} %bitcast.72, bf16[1536,2048]{1,0:T(8,128)(2,1)} %subtract_convert_fusion.cols_ref, bf16[1536,512]{1,0:T(8,128)(2,1)S(1)} %pad_maximum_fusion.q_ref, ...), custom_call_target="tpu_custom_call" | custom-call | tf_op jit(solution)/shard_map/pallas_call | solution.py:253
  (6 shorter events, 0.0 us)
Async XLA Ops:
  37.9 0.9 copy-start.2
  61.5 1.7 %copy-start.3 = (bf16[96,16,128,2]{2,3,1,0:T(2,128)(2,1)S(1)}, bf16[96,16,128,2]{2,3,1,0:T(2,128)(2,1)}, u32[]{:S(2)}) copy-start(bf16[96,16,128,2]{2,3,1,0:T(2,128)(2,1)} %copy-done.2) | copy-start | bytes 2359300
  69.9 1.8 %copy-start = (f32[256,256]{1,0:T(8,128)S(1)}, f32[256,256]{1,0:T(8,128)}, u32[]{:S(2)}) copy-start(f32[256,256]{1,0:T(8,128)} %get-tuple-element.11.edge_ref) | copy-start | bytes 786436
  74.6 5.8 %copy-start.1 = (f32[4096]{0:T(1024)S(1)}, f32[4096]{0:T(1024)}, u32[]{:S(2)}) copy-start(f32[4096]{0:T(1024)} %param.5) | copy-start | bytes 49156

commit v3 on v2

--- a/solution.py
+++ b/solution.py
@@ -152,12 +152,13 @@
 
 
 def assemble_kernel(
-    comm, row_tiles, col_tiles, ids_ref, at_ref, blocks_ref, cols_ref, q_ref, top_ref, edge_ref,
+    comm, pairs, col_tiles, ids_ref, at_ref, blocks_ref, cols_ref, q_ref, top_ref, edge_ref,
     bar_ref, rest_ref, panel_ref, left, right, lists, counts,
 ):
     step = pl.program_id(0)
     row_first, col_first = at_ref[0], at_ref[1]
     band = col_tiles * TILE
+    room = PANELS * comm
 
     @pl.when(step == 0)
     def _():
@@ -168,21 +169,22 @@
             counts[i] = 0
             return 0
 
-        lax.fori_loop(0, row_tiles + 1, clear, 0)
+        lax.fori_loop(0, pairs + 1, clear, 0)
 
         def enter(k, _):
             for s in range(BT):
                 where = ids_ref[k * BT + s] - row_first
-                inside = jnp.logical_and(where >= 0, where < row_tiles)
-                where = jnp.where(inside, where, row_tiles)
-                n = counts[where]
-                lists[where * comm + jnp.minimum(n, comm - 1)] = k * BT + s
-                counts[where] = n + 1
+                inside = jnp.logical_and(where >= 0, where < pairs * PANELS)
+                pair = jnp.where(inside, where >> 1, pairs)
+                n = counts[pair]
+                entry = (k * BT + s) * PANELS + (where & 1)
+                lists[pair * room + jnp.minimum(n, room - 1)] = entry
+                counts[pair] = n + 1
             return 0
 
         lax.fori_loop(0, comm, enter, 0)
 
-    tile = row_first + step
+    tile = row_first + step * PANELS
     total = counts[step]
 
     def pick(chunk):
@@ -190,11 +192,13 @@
         some = jnp.minimum(total - base, GROUP)
 
         def one(j, _):
-            entry = lists[step * comm + base + j]
-            k, s = entry // BT, entry % BT
+            entry = lists[step * room + base + j]
+            k, s, half = entry >> 4, (entry >> 1) & 7, entry & 1
             src = pl.ds(pl.multiple_of(k * COLS, COLS), COLS)
             dst = pl.ds(pl.multiple_of(j * COLS, COLS), COLS)
-            left[dst, :] = blocks_ref[src, pl.ds(pl.multiple_of(s * TILE, TILE), TILE)]
+            block = blocks_ref[src, pl.ds(pl.multiple_of(s * TILE, TILE), TILE)]
+            left[dst, pl.ds(pl.multiple_of(half * TILE, TILE), TILE)] = block
+            left[dst, pl.ds(pl.multiple_of((1 - half) * TILE, TILE), TILE)] = jnp.zeros_like(block)
             right[dst, :band] = cols_ref[src, :]
             right[dst, band:] = q_ref[src, :]
             return 0
@@ -203,68 +207,68 @@
 
         def blank(j, _):
             dst = pl.ds(pl.multiple_of(j * COLS, COLS), COLS)
-            left[dst, :] = jnp.zeros((COLS, TILE), left.dtype)
+            left[dst, :] = jnp.zeros((COLS, WIDE), left.dtype)
             return 0
 
         lax.fori_loop(some, GROUP, blank, 0)
 
-    def times():
-        return lax.dot_general(
-            left[...], right[...], (((0,), (0,)), ((), ())), preferred_element_type=jnp.float32
-        )
+    def times(rows, at):
+        return jnp.dot(rows, right[:, at : at + WIDE], preferred_element_type=jnp.float32)
 
     @pl.when(tile >= PANELS)
     def _():
         pick(0)
-        got = times()
-        rest_ref[...] = got[:, :band]
-        panel_ref[...] = got[:, band : band + WIDE] + got[:, band + WIDE :]
+        rows = left[...].T
+        for at in range(0, band, WIDE):
+            rest_ref[:, at : at + WIDE] = times(rows, at)
+        panel_ref[...] = times(rows, band) + times(rows, band + WIDE)
 
         def more(chunk, _):
             pick(chunk)
-            got = times()
-            rest_ref[...] += got[:, :band]
-            panel_ref[...] += got[:, band : band + WIDE] + got[:, band + WIDE :]
+            rows = left[...].T
+            for at in range(0, band, WIDE):
+                rest_ref[:, at : at + WIDE] += times(rows, at)
+            panel_ref[...] += times(rows, band) + times(rows, band + WIDE)
             return 0
 
         lax.fori_loop(1, (total + GROUP - 1) // GROUP, more, 0)
 
     @pl.when(tile < PANELS)
     def _():
-        src = pl.ds(pl.multiple_of(jnp.minimum(tile, PANELS - 1) * TILE, TILE), TILE)
-        rest_ref[...] = top_ref[src, :]
-        panel_ref[...] = edge_ref[src, :]
+        rest_ref[...] = top_ref[...]
+        panel_ref[...] = edge_ref[...]
 
     own = tile - col_first
 
     @pl.when(jnp.logical_and(own >= 0, own < col_tiles))
     def _():
         line = bar_ref[pl.ds(step, 1), :]
-        there = lax.broadcasted_iota(jnp.int32, (TILE, TILE), 0)
-        here = lax.broadcasted_iota(jnp.int32, (TILE, TILE), 1)
-        spot = pl.ds(pl.multiple_of(own * TILE, TILE), TILE)
-        rest_ref[:, spot] += jnp.where(there == here, jnp.broadcast_to(line, (TILE, TILE)), 0.0)
+        there = lax.broadcasted_iota(jnp.int32, (WIDE, WIDE), 0)
+        here = lax.broadcasted_iota(jnp.int32, (WIDE, WIDE), 1)
+        spot = pl.ds(pl.multiple_of(own * TILE, WIDE), WIDE)
+        rest_ref[:, spot] += jnp.where(there == here, jnp.broadcast_to(line, (WIDE, WIDE)), 0.0)
 
 
 def assemble(ids, at, blocks, cols, q, top, edge, bar, row_tiles, col_tiles):
     comm = ids.shape[0] // BT
     band = col_tiles * TILE
+    pairs = row_tiles // PANELS
     whole = pl.BlockSpec(memory_space=pltpu.VMEM)
     return pl.pallas_call(
-        functools.partial(assemble_kernel, comm, row_tiles, col_tiles),
+        functools.partial(assemble_kernel, comm, pairs, col_tiles),
         grid_spec=pltpu.PrefetchScalarGridSpec(
             num_scalar_prefetch=2,
-            grid=(row_tiles,),
+            grid=(pairs,),
             in_specs=[whole] * 6,
             out_specs=[
-                pl.BlockSpec((TILE, band), lambda i, *_: (i, 0)),
-                pl.BlockSpec((TILE, WIDE), lambda i, *_: (i, 0)),
+                pl.BlockSpec((WIDE, band), lambda i, *_: (i, 0)),
+                pl.BlockSpec((WIDE, WIDE), lambda i, *_: (i, 0)),
             ],
             scratch_shapes=[
-                pltpu.VMEM((GROUP * COLS, TILE), jnp.bfloat16),
+                pltpu.VMEM((GROUP * COLS, WIDE), jnp.bfloat16),
                 pltpu.VMEM((GROUP * COLS, band + q.shape[1]), jnp.bfloat16),
-                pltpu.SMEM(((row_tiles + 1) * comm,), jnp.int32),
-                pltpu.SMEM((row_tiles + 1,), jnp.int32),
+                pltpu.SMEM(((pairs + 1) * PANELS * comm,), jnp.int32),
+                pltpu.SMEM((pairs + 1,), jnp.int32),
             ],
         ),
         out_shape=[
@@ -392,7 +396,7 @@
     top = top - jnp.concatenate([jnp.zeros_like(lower), lower], axis=0)
     at = jnp.stack([row_first, col_first]).astype(jnp.int32)
     rest, panels = assemble(
-        ids, at, rows, rhs, qs, top, edge, barrier.reshape(row_tiles, TILE), row_tiles, col_tiles
+        ids, at, rows, rhs, qs, top, edge, barrier.reshape(row_tiles // PANELS, WIDE), row_tiles, col_tiles
     )
     return panels, rest
 

time: 116 us -> 113 us (0.974)
  Pallas kernels: 86.3 us -> 83 us
    pallas_call x1, Pallas kernels: 34.4 us -> 31.2 us  [assemble(): pl.pallas_call(functools.partial(assemble_kernel, comm, pairs, col_tiles)...]
    unnamed x10 -> x8, local copies, waits for them, and re-layouts: 4.52 us -> 4.52 us
where the time goes in v3:
time: 113 us; the launch traced here: 112 us
  Pallas kernels  83 us (73%)
  matrix products  21 us (19%)
  local copies, waits for them, and re-layouts  6.17 us (5%)
  other arithmetic  1.57 us (1%)
    pallas_call x1, Pallas kernels, assemble(): pl.pallas_call(functools.partial(assemble_kernel, comm, pairs, col_tiles)...  31.2 us
    pallas_call x1, Pallas kernels, gather_all(): pl.pallas_call(functools.partial(gather_kernel, sizes), out_shape=(jax.Sh...  30.2 us
    pallas_call x1, Pallas kernels, factor(): pl.pallas_call(factor_kernel, out_shape=[jax.ShapeDtypeStruct(corner.shap...  21.6 us
    dot_general x7, matrix products, mul(): lax.dot_general(lhs, rhs, (((left,), (right,)), ((), ())), precision=prec...  14.8 us
    dot_general x2, matrix products, expand(): jnp.einsum('kas,kjai->kjsi', onehot, tiled, preferred_element_type=jnp.fl...  6.18 us
    unnamed x8, local copies, waits for them, and re-layouts  4.52 us

profile of v3, /device:TPU:9, one launch (start us, length us, event | category | flops | bytes accessed | tf_op | source)
XLA Modules:
  0.0 112.5 jit_solution(8023998128965701969)
XLA Ops:
  0.6 0.1 pad_add_fusion.at_ref
  0.7 0.7 slice.15
  1.4 0.7 convert_element_type.44
  2.1 0.1 convert_element_type.45
  2.2 0.7 maximum_bitcast_fusion.s_ref
  2.9 0.7 reshape.120.bar_ref
  3.6 30.2 %shard_map.50 = (bf16[32,48,1024]{2,1,0:T(8,128)(2,1)}, f32[32,8,128]{2,1,0:T(8,128)}) custom-call(bf16[48,1024]{1,0:T(8,128)(2,1)} %bitcast.78, f32[8,128]{1,0:T(8,128)} %maximum_bitcast_fusion.s_ref), custom_call_target="tpu_custom_call" | custom-call | tf_op jit(solution)/shard_map/pallas_call | solution.py:137
  33.8 0.9 copy.49
  34.8 0.1 reshape.116.ids_ref
  34.9 0.1 eq.32
  34.9 2.7 %copy.14 = bf16[192,8,8,128]{3,2,1,0:T(8,128)(2,1)S(1)} copy(bf16[192,8,8,128]{3,1,2,0:T(8,128)(2,1)} %bitcast.69) | data formatting | bytes 6291456
  37.7 1.0 fusion.16
  38.7 0.0 copy-start.1
  38.7 0.9 copy-done.1
  39.5 1.1 convolution_add_fusion.1.corner_ref
  40.7 21.6 %shard_map.51 = (f32[256,256]{1,0:T(8,128)}, f32[256,256]{1,0:T(8,128)}) custom-call(f32[256,256]{1,0:T(8,128)} %convolution_add_fusion.1.corner_ref), custom_call_target="tpu_custom_call" | custom-call | tf_op jit(solution)/shard_map/pallas_call | solution.py:327
  62.2 0.0 copy-start.2
  62.2 1.7 %fusion.24 = f32[1536,256]{1,0:T(8,128)S(1)} fusion(bf16[192,8,2,128]{3,2,1,0:T(2,128)(2,1)} %bitcast.72, f32[256,256]{1,0:T(8,128)} %get-tuple-element.10), kind=kOutput, calls=%fused_computation.25 | convolution fusion | flops 201457664 | bytes 2621440 | tf_op jit(solution)/shard_map/dot_general | solution.py:346
  63.9 0.0 copy-done.2
  63.9 1.4 %fusion.15 = (bf16[1536,256]{1,0:T(8,128)(2,1)S(1)}, bf16[1536,256]{1,0:T(8,128)(2,1)S(1)}) fusion(f32[1536,256]{1,0:T(8,128)S(1)} %fusion.24, f32[256,256]{1,0:T(8,128)} %get-tuple-element.10, bf16[192,8,2,128]{3,2,1,0:T(2,128)(2,1)S(1)} %bitcast.73), kind=kOutput, calls=%fused_computation.16 | convolution fusion | flops 203489280 | bytes 4194304 | tf_op jit(solution)/shard_map/dot_general | solution.py:346
  65.3 0.1 pad_maximum_fusion.q_ref
  65.4 5.2 %convolution_convert_fusion = bf16[96,16,128,16]{2,3,1,0:T(8,128)(2,1)S(1)} fusion(s32[16]{0:T(128)S(1)} %iota_add_fusion, s32[96,8]{1,0:T(8,128)S(1)} %eq.32, bf16[96,16,8,128]{3,2,1,0:T(8,128)(2,1)S(1)} %bitcast.68), kind=kOutput, calls=%fused_computation.7 | convolution fusion | flops 53489664 | bytes 9440320 | tf_op jit(solution)/shard_map/kas,kjai->kjsi/dot_general | solution.py:339
  70.6 0.0 copy-start
  70.6 1.8 %fusion.12 = f32[256,2048]{1,0:T(8,128)S(1)} fusion(bf16[1536,256]{1,0:T(8,128)(2,1)S(1)} %get-tuple-element.15, bf16[192,8,16,128]{3,2,1,0:T(8,128)(2,1)S(1)} %bitcast.64, s32[2048]{0:T(1024)S(1)} %fusion.42, s32[256]{0:T(256)S(1)} %and_select_fusion), kind=kOutput, calls=%fused_computation.13 | convolution fusion | flops 1611661312 | bytes 9184256 | tf_op jit(solution)/shard_map/dot_general | solution.py:346
  72.4 0.0 copy-done
  72.4 1.0 fusion.19
  73.5 1.8 %fusion.9.top_ref = f32[256,2048]{1,0:T(8,128)S(1)} fusion(bf16[192,8,16,128]{3,2,1,0:T(8,128)(2,1)S(1)} %bitcast.65, f32[128,2048]{1,0:T(8,128)S(1)} %fusion.19, bf16[192,8,2,128]{3,2,1,0:T(2,128)(2,1)S(1)} %bitcast.74), kind=kOutput, calls=%fused_computation.12 | convolution fusion | flops 1611137024 | bytes 10223616 | tf_op jit(solution)/shard_map/dot_general | solution.py:346
  75.3 6.0 %subtract_convert_fusion.cols_ref = bf16[1536,2048]{1,0:T(8,128)(2,1)} fusion(bf16[1536,256]{1,0:T(8,128)(2,1)S(1)} %get-tuple-element.15, bf16[192,8,16,128]{3,2,1,0:T(8,128)(2,1)S(1)} %bitcast.66, f32[256,2048]{1,0:T(8,128)S(1)} %fusion.12), kind=kOutput, calls=%fused_computation | convolution fusion | flops 1620574208 | bytes 15466496 | tf_op jit(solution)/shard_map/dot_general | solution.py:346
  81.3 31.2 %shard_map.52 = (f32[4096,2048]{1,0:T(8,128)}, f32[4096,256]{1,0:T(8,128)}) custom-call(s32[768]{0:T(1024)S(1)} %reshape.116.ids_ref, s32[2]{0:T(128)S(1)} %pad_add_fusion.at_ref, bf16[1536,1024]{1,0:T(8,128)(2,1)} %bitcast.70, bf16[1536,2048]{1,0:T(8,128)(2,1)} %subtract_convert_fusion.cols_ref, bf16[1536,512]{1,0:T(8,128)(2,1)S(1)} %pad_maximum_fusion.q_ref, ...), custom_call_target="tpu_custom_call" | custom-call | tf_op jit(solution)/shard_map/pallas_call | solution.py:257
  (6 shorter events, 0.0 us)
Async XLA Ops:
  38.7 0.9 copy-start.1
  62.2 1.7 %copy-start.2 = (bf16[96,16,128,2]{2,3,1,0:T(2,128)(2,1)S(1)}, bf16[96,16,128,2]{2,3,1,0:T(2,128)(2,1)}, u32[]{:S(2)}) copy-start(bf16[96,16,128,2]{2,3,1,0:T(2,128)(2,1)} %copy-done.1) | copy-start | bytes 2359300
  70.6 1.8 %copy-start = (f32[256,256]{1,0:T(8,128)S(1)}, f32[256,256]{1,0:T(8,128)}, u32[]{:S(2)}) copy-start(f32[256,256]{1,0:T(8,128)} %get-tuple-element.11.edge_ref) | copy-start | bytes 786436

commit v4 on v3

--- a/solution.py
+++ b/solution.py
@@ -182,7 +182,7 @@
                 counts[pair] = n + 1
             return 0
 
-        lax.fori_loop(0, comm, enter, 0)
+        lax.fori_loop(0, comm, enter, 0, unroll=4)
 
     tile = row_first + step * PANELS
     total = counts[step]

time: 113 us -> 111 us (0.982)
  Pallas kernels: 83 us -> 81.3 us
    pallas_call x1, Pallas kernels: 31.2 us -> 29.5 us  [assemble(): pl.pallas_call(functools.partial(assemble_kernel, comm, pairs, col_tiles)...]
where the time goes in v4:
time: 111 us
  Pallas kernels  81.3 us (73%)
  matrix products  21 us (19%)
  local copies, waits for them, and re-layouts  6.17 us (6%)
  other arithmetic  1.57 us (1%)
    pallas_call x1, Pallas kernels, gather_all(): pl.pallas_call(functools.partial(gather_kernel, sizes), out_shape=(jax.Sh...  30.2 us
    pallas_call x1, Pallas kernels, assemble(): pl.pallas_call(functools.partial(assemble_kernel, comm, pairs, col_tiles)...  29.5 us
    pallas_call x1, Pallas kernels, factor(): pl.pallas_call(factor_kernel, out_shape=[jax.ShapeDtypeStruct(corner.shap...  21.6 us
    dot_general x7, matrix products, mul(): lax.dot_general(lhs, rhs, (((left,), (right,)), ((), ())), precision=prec...  14.8 us
    dot_general x2, matrix products, expand(): jnp.einsum('kas,kjai->kjsi', onehot, tiled, preferred_element_type=jnp.fl...  6.18 us
    unnamed x8, local copies, waits for them, and re-layouts  4.52 us

profile of v4, /device:TPU:9, one launch (start us, length us, event | category | flops | bytes accessed | tf_op | source)
XLA Modules:
  0.0 110.8 jit_solution(14657222847749380797)
XLA Ops:
  0.6 0.1 pad_add_fusion.at_ref
  0.7 0.7 slice.15
  1.4 0.7 convert_element_type.44
  2.1 0.1 convert_element_type.45
  2.2 0.7 maximum_bitcast_fusion.s_ref
  2.9 0.7 reshape.120.bar_ref
  3.6 30.2 %shard_map.50 = (bf16[32,48,1024]{2,1,0:T(8,128)(2,1)}, f32[32,8,128]{2,1,0:T(8,128)}) custom-call(bf16[48,1024]{1,0:T(8,128)(2,1)} %bitcast.78, f32[8,128]{1,0:T(8,128)} %maximum_bitcast_fusion.s_ref), custom_call_target="tpu_custom_call" | custom-call | tf_op jit(solution)/shard_map/pallas_call | solution.py:137
  33.8 0.9 copy.49
  34.8 0.1 reshape.116.ids_ref
  34.9 0.1 eq.32
  34.9 2.7 %copy.14 = bf16[192,8,8,128]{3,2,1,0:T(8,128)(2,1)S(1)} copy(bf16[192,8,8,128]{3,1,2,0:T(8,128)(2,1)} %bitcast.69) | data formatting | bytes 6291456
  37.7 1.0 fusion.16
  38.7 0.0 copy-start.1
  38.7 0.9 copy-done.1
  39.5 1.1 %convolution_add_fusion.1.corner_ref = f32[256,256]{1,0:T(8,128)} fusion(bf16[192,8,2,128]{3,2,1,0:T(2,128)(2,1)S(1)} %bitcast.71, f32[256]{0:T(256)S(1)} %bitcast.79), kind=kOutput, calls=%fused_computation.19 | convolution fusion | flops 201523200 | bytes 1049600 | tf_op jit(solution)/shard_map/dot_general | solution.py:346
  40.7 21.6 %shard_map.51 = (f32[256,256]{1,0:T(8,128)}, f32[256,256]{1,0:T(8,128)}) custom-call(f32[256,256]{1,0:T(8,128)} %convolution_add_fusion.1.corner_ref), custom_call_target="tpu_custom_call" | custom-call | tf_op jit(solution)/shard_map/pallas_call | solution.py:327
  62.2 0.0 copy-start.2
  62.2 1.7 %fusion.24 = f32[1536,256]{1,0:T(8,128)S(1)} fusion(bf16[192,8,2,128]{3,2,1,0:T(2,128)(2,1)} %bitcast.72, f32[256,256]{1,0:T(8,128)} %get-tuple-element.10), kind=kOutput, calls=%fused_computation.25 | convolution fusion | flops 201457664 | bytes 2621440 | tf_op jit(solution)/shard_map/dot_general | solution.py:346
  63.9 0.0 copy-done.2
  63.9 1.4 %fusion.15 = (bf16[1536,256]{1,0:T(8,128)(2,1)S(1)}, bf16[1536,256]{1,0:T(8,128)(2,1)S(1)}) fusion(f32[1536,256]{1,0:T(8,128)S(1)} %fusion.24, f32[256,256]{1,0:T(8,128)} %get-tuple-element.10, bf16[192,8,2,128]{3,2,1,0:T(2,128)(2,1)S(1)} %bitcast.73), kind=kOutput, calls=%fused_computation.16 | convolution fusion | flops 203489280 | bytes 4194304 | tf_op jit(solution)/shard_map/dot_general | solution.py:346
  65.3 0.1 pad_maximum_fusion.q_ref
  65.4 5.2 %convolution_convert_fusion = bf16[96,16,128,16]{2,3,1,0:T(8,128)(2,1)S(1)} fusion(s32[16]{0:T(128)S(1)} %iota_add_fusion, s32[96,8]{1,0:T(8,128)S(1)} %eq.32, bf16[96,16,8,128]{3,2,1,0:T(8,128)(2,1)S(1)} %bitcast.68), kind=kOutput, calls=%fused_computation.7 | convolution fusion | flops 53489664 | bytes 9440320 | tf_op jit(solution)/shard_map/kas,kjai->kjsi/dot_general | solution.py:339
  70.6 0.0 copy-start
  70.6 1.8 %fusion.12 = f32[256,2048]{1,0:T(8,128)S(1)} fusion(bf16[1536,256]{1,0:T(8,128)(2,1)S(1)} %get-tuple-element.15, bf16[192,8,16,128]{3,2,1,0:T(8,128)(2,1)S(1)} %bitcast.64, s32[2048]{0:T(1024)S(1)} %fusion.42, s32[256]{0:T(256)S(1)} %and_select_fusion), kind=kOutput, calls=%fused_computation.13 | convolution fusion | flops 1611661312 | bytes 9184256 | tf_op jit(solution)/shard_map/dot_general | solution.py:346
  72.4 0.0 copy-done
  72.4 1.0 fusion.19
  73.5 1.8 %fusion.9.top_ref = f32[256,2048]{1,0:T(8,128)S(1)} fusion(bf16[192,8,16,128]{3,2,1,0:T(8,128)(2,1)S(1)} %bitcast.65, f32[128,2048]{1,0:T(8,128)S(1)} %fusion.19, bf16[192,8,2,128]{3,2,1,0:T(2,128)(2,1)S(1)} %bitcast.74), kind=kOutput, calls=%fused_computation.12 | convolution fusion | flops 1611137024 | bytes 10223616 | tf_op jit(solution)/shard_map/dot_general | solution.py:346
  75.3 6.0 %subtract_convert_fusion.cols_ref = bf16[1536,2048]{1,0:T(8,128)(2,1)} fusion(bf16[1536,256]{1,0:T(8,128)(2,1)S(1)} %get-tuple-element.15, bf16[192,8,16,128]{3,2,1,0:T(8,128)(2,1)S(1)} %bitcast.66, f32[256,2048]{1,0:T(8,128)S(1)} %fusion.12), kind=kOutput, calls=%fused_computation | convolution fusion | flops 1620574208 | bytes 15466496 | tf_op jit(solution)/shard_map/dot_general | solution.py:346
  81.3 29.5 %shard_map.52 = (f32[4096,2048]{1,0:T(8,128)}, f32[4096,256]{1,0:T(8,128)}) custom-call(s32[768]{0:T(1024)S(1)} %reshape.116.ids_ref, s32[2]{0:T(128)S(1)} %pad_add_fusion.at_ref, bf16[1536,1024]{1,0:T(8,128)(2,1)} %bitcast.70, bf16[1536,2048]{1,0:T(8,128)(2,1)} %subtract_convert_fusion.cols_ref, bf16[1536,512]{1,0:T(8,128)(2,1)S(1)} %pad_maximum_fusion.q_ref, ...), custom_call_target="tpu_custom_call" | custom-call | tf_op jit(solution)/shard_map/pallas_call | solution.py:257
  (6 shorter events, 0.0 us)
Async XLA Ops:
  38.7 0.9 copy-start.1
  62.2 1.7 %copy-start.2 = (bf16[96,16,128,2]{2,3,1,0:T(2,128)(2,1)S(1)}, bf16[96,16,128,2]{2,3,1,0:T(2,128)(2,1)}, u32[]{:S(2)}) copy-start(bf16[96,16,128,2]{2,3,1,0:T(2,128)(2,1)} %copy-done.1) | copy-start | bytes 2359300
  70.6 1.8 %copy-start = (f32[256,256]{1,0:T(8,128)S(1)}, f32[256,256]{1,0:T(8,128)}, u32[]{:S(2)}) copy-start(f32[256,256]{1,0:T(8,128)} %get-tuple-element.11.edge_ref) | copy-start | bytes 786436
